TPU v7x, 32 devices: a whole 2x2x4 slice. The times are simulated.
32 devices in a mesh: space: 4 (over y, core), vel: 8 (over z, x).
Axes of the slice: x: 2, y: 2, z: 4, core: 2. Of those that a mesh axis runs over, the one named last changes fastest.
Arguments:
- distribution: float32 [32768, 16, 128], P('vel', 'space'), may hold values from -6 to 6
- velocity_order: int32 [32768], P('vel'), may hold values from 0 to 32767, as said below
- macro_state: float32 [13, 16, 128], P(None, 'space'), may hold values from -5 to 5
- rarefaction: float32 [16, 128], P('space'), may hold values from 0.1 to 3
- wall_mask: int32 [16, 128], P('space'), may hold values from 0 to 2, as said below
Outputs:
- dist_out: float32 [32768, 16, 128], P('vel', 'space')
- moments_out: float32 [13, 16, 128], P(None, 'space')
Inputs may be any that keep to these rules, and one draw needn't show every extreme that they name: `velocity_order`: A permutation of the velocity indices. In each shard of 4096 consecutive slots along vel, the first 2048 slots hold indices of at least 16384 and the others indices below 16384. `wall_mask`: cells on the faces x = 0, x = 15, y = 0, z = 0 and z = 7 are 1; the other cells of the face y = 15 are 2; some interior cells are 1.
All inputs are finite; a program needn't handle non-finite values.
Results may differ from a plain program's by a relative error of at most 0.0003.
Values sent between devices are 32-bit elements; how exact they have to be, the bound alone decides.
A program may use at most 64 MiB of HBM per device.

v0:
```python
import jax
import jax.numpy as jnp
from jax import lax
from jax.sharding import PartitionSpec as P

NQ = 32
NZ = 8
SWEEPS = 4


VELOCITY_RANGE = 4.0
LID_SPEED = 1.0
DIFFUSION = 1.0
REACTION = 1.0
COUPLING = (
    (0, 1, 0, 0.24),
    (0, 2, 1, 0.24),
    (0, 3, 2, 0.24),
    (1, 0, 0, 0.2),
    (1, 4, 0, 0.2),
    (1, 5, 0, 0.2),
    (1, 7, 1, 0.1),
    (1, 8, 2, 0.1),
    (2, 0, 1, 0.2),
    (2, 4, 1, 0.2),
    (2, 6, 1, 0.2),
    (2, 7, 0, 0.1),
    (2, 9, 2, 0.1),
    (3, 0, 2, 0.2),
    (3, 4, 2, 0.2),
    (3, 8, 0, 0.1),
    (3, 9, 1, 0.1),
    (4, 10, 0, 0.2),
    (4, 11, 1, 0.2),
    (4, 12, 2, 0.2),
    (5, 1, 0, 0.4),
    (5, 10, 0, 0.2),
    (6, 2, 1, 0.4),
    (6, 11, 1, 0.2),
    (7, 1, 1, 0.2),
    (7, 2, 0, 0.2),
    (8, 1, 2, 0.2),
    (8, 3, 0, 0.2),
    (9, 2, 2, 0.2),
    (9, 3, 1, 0.2),
    (10, 4, 0, 0.5),
    (10, 5, 0, 0.2),
    (11, 4, 1, 0.5),
    (11, 6, 1, 0.2),
    (12, 4, 2, 0.5),
    (12, 8, 0, 0.1),
    (12, 9, 1, 0.1),
)


def padded_2(cells, sides, width):
    for axis, dim in sides:
        count = lax.axis_size(axis)
        ends = count - 1
        head = lax.slice_in_dim(cells, 0, width, axis=dim)
        tail = lax.slice_in_dim(cells, cells.shape[dim] - width, cells.shape[dim], axis=dim)
        cells = jnp.concatenate(
            [
                lax.ppermute(tail, axis, [(i, (i + 1) % count) for i in range(ends)]),
                cells,
                lax.ppermute(head, axis, [((i + 1) % count, i) for i in range(ends)]),
            ],
            axis=dim,
        )
    return cells


def coupling_tables(dtype):
    coupling_table = [
        [[0.0 for column_index in range(13)] for row_index in range(13)] for dim_index in range(3)
    ]
    for row_index, column_index, dim_index, value in COUPLING:
        coupling_table[dim_index][row_index][column_index] = value
    return jnp.asarray(coupling_table, dtype=dtype)


def velocity_tables(velocity_order, points):
    first_index = velocity_order // (points * points)
    second_index = velocity_order // points % points
    third_index = velocity_order % points

    def velocity_axis(index_value):
        return VELOCITY_RANGE * (2.0 * index_value.astype(jnp.float32) + 1.0 - points) / points

    xi_x = velocity_axis(first_index)
    xi_y = velocity_axis(second_index)
    xi_z = velocity_axis(third_index)
    square = xi_x * xi_x + xi_y * xi_y + xi_z * xi_z
    quad_weight = (2.0 * VELOCITY_RANGE / points) ** 3 * jnp.exp(-square) / jnp.pi**1.5
    unit_row = jnp.ones_like(square)
    zero_row = jnp.zeros_like(square)
    energy = square - 1.5
    heat_factor = square - 2.5
    moment_rows = (
        jnp.stack(
            [
                unit_row,
                xi_x,
                xi_y,
                xi_z,
                2.0 / 3.0 * energy,
                2.0 * (xi_x * xi_x - square / 3.0),
                2.0 * (xi_y * xi_y - square / 3.0),
                2.0 * xi_x * xi_y,
                2.0 * xi_x * xi_z,
                2.0 * xi_y * xi_z,
                xi_x * heat_factor,
                xi_y * heat_factor,
                xi_z * heat_factor,
            ]
        )
        * quad_weight[None]
    )
    shakhov = 4.0 / 15.0
    equilibrium_rows = jnp.stack(
        [
            unit_row,
            2.0 * xi_x,
            2.0 * xi_y,
            2.0 * xi_z,
            energy,
            zero_row,
            zero_row,
            zero_row,
            zero_row,
            zero_row,
            shakhov * xi_x * heat_factor,
            shakhov * xi_y * heat_factor,
            shakhov * xi_z * heat_factor,
        ]
    )
    grad_rows = jnp.stack(
        [
            unit_row,
            2.0 * xi_x,
            2.0 * xi_y,
            2.0 * xi_z,
            energy,
            xi_x * xi_x - xi_z * xi_z,
            xi_y * xi_y - xi_z * xi_z,
            2.0 * xi_x * xi_y,
            2.0 * xi_x * xi_z,
            2.0 * xi_y * xi_z,
            0.8 * xi_x * heat_factor,
            0.8 * xi_y * heat_factor,
            0.8 * xi_z * heat_factor,
        ]
    )
    return (xi_x, xi_y, xi_z, moment_rows, equilibrium_rows, grad_rows)


def relax(padded, held_moments, reaction, gas_cells, coupling):
    upper_x = padded[:, 2:, 1:-1, 1:-1]
    lower_x = padded[:, :-2, 1:-1, 1:-1]
    upper_y = padded[:, 1:-1, 2:, 1:-1]
    lower_y = padded[:, 1:-1, :-2, 1:-1]
    upper_z = padded[:, 1:-1, 1:-1, 2:]
    lower_z = padded[:, 1:-1, 1:-1, :-2]
    beside_all = upper_x + lower_x + upper_y + lower_y + upper_z + lower_z
    coupled = (
        jnp.einsum("kl,lxyz->kxyz", coupling[0], upper_x - lower_x, precision=lax.Precision.HIGHEST)
        + jnp.einsum(
            "kl,lxyz->kxyz", coupling[1], upper_y - lower_y, precision=lax.Precision.HIGHEST
        )
        + jnp.einsum(
            "kl,lxyz->kxyz", coupling[2], upper_z - lower_z, precision=lax.Precision.HIGHEST
        )
    )
    updated = (reaction * held_moments + DIFFUSION * beside_all - 0.5 * coupled) / (
        reaction + 6.0 * DIFFUSION
    )
    return jnp.where(gas_cells, updated, held_moments)


def local(distribution, velocity_order, macro_state, rarefaction, wall_mask):
    slot_count, width_x, plane_size = distribution.shape
    half_count = slot_count // 2
    rows_y = plane_size // NZ
    xi_x, xi_y, xi_z, moment_rows, equilibrium_rows, grad_rows = velocity_tables(velocity_order, NQ)
    is_wall = wall_mask != 0
    moving = (wall_mask == 2).astype(jnp.float32)
    wall_state = macro_state[0][None] + 2.0 * LID_SPEED * moving[None] * xi_x[:, None, None]
    current = jnp.where(is_wall[None], wall_state, distribution)
    extended = padded_2(current, (("space", 1),), 1)
    along_x = jnp.concatenate([extended[:half_count, :-2], extended[half_count:, 2:]], axis=0)
    z_index = jnp.arange(plane_size, dtype=jnp.int32) % NZ
    lower_y = jnp.pad(current, ((0, 0), (0, 0), (NZ, 0)))[:, :, :plane_size]
    upper_y = jnp.pad(current, ((0, 0), (0, 0), (0, NZ)))[:, :, NZ:]
    lower_z = jnp.where(
        z_index != 0, jnp.pad(current, ((0, 0), (0, 0), (1, 0)))[:, :, :plane_size], 0.0
    )
    upper_z = jnp.where(
        z_index != NZ - 1, jnp.pad(current, ((0, 0), (0, 0), (0, 1)))[:, :, 1:], 0.0
    )
    speed_x = xi_x[:, None, None]
    speed_y = xi_y[:, None, None]
    speed_z = xi_z[:, None, None]
    upwind = (
        jnp.abs(speed_x) * along_x
        + jnp.abs(speed_y) * jnp.where(speed_y > 0, lower_y, upper_y)
        + jnp.abs(speed_z) * jnp.where(speed_z > 0, lower_z, upper_z)
    )
    eq_state = jnp.dot(
        equilibrium_rows.T, macro_state.reshape(13, -1), precision=lax.Precision.HIGHEST
    ).reshape(slot_count, width_x, plane_size)
    rate_field = rarefaction[None]
    denominator = rate_field + jnp.abs(speed_x) + jnp.abs(speed_y) + jnp.abs(speed_z)
    updated = jnp.where(is_wall[None], wall_state, (rate_field * eq_state + upwind) / denominator)
    partial_value = jnp.dot(
        moment_rows, updated.reshape(slot_count, -1), precision=lax.Precision.HIGHEST
    ).reshape(13, width_x, plane_size)
    reaction_full = REACTION * (1.0 + rarefaction)
    gas_full = jnp.logical_not(is_wall)
    coupling = coupling_tables(partial_value.dtype)
    held_moments = lax.psum(partial_value, "vel").reshape(13, width_x, rows_y, NZ)
    reaction = reaction_full.reshape(1, width_x, rows_y, NZ)
    gas_cells = gas_full.reshape(1, width_x, rows_y, NZ)
    moments_now = held_moments
    for sweep_index in range(SWEEPS):
        extended_moments = padded_2(moments_now, (("space", 1),), 1)
        padded = jnp.pad(extended_moments, ((0, 0), (0, 0), (1, 1), (1, 1)))
        moments_now = relax(padded, held_moments, reaction, gas_cells, coupling)
    settled = moments_now.reshape(13, width_x, plane_size)
    change = (moments_now - held_moments).reshape(13, width_x, plane_size)
    correction = jnp.dot(
        grad_rows.T, change.reshape(13, -1), precision=lax.Precision.HIGHEST
    ).reshape(slot_count, width_x, plane_size)
    return (updated + correction, settled)


def solution(mesh):
    return jax.shard_map(
        local,
        mesh=mesh,
        in_specs=(
            P("vel", "space", None),
            P("vel"),
            P(None, "space", None),
            P("space", None),
            P("space", None),
        ),
        out_specs=(P("vel", "space", None), P(None, "space", None)),
        check_vma=False,
    )
```

profile of v0, /device:TPU:1, one launch (start us, length us, event | category | flops | bytes accessed | tf_op | source)
XLA Modules:
  0.0 189.1 jit_solution(14837909189211507533)
XLA Ops:
  0.6 0.7 fusion.86
  1.3 0.7 compare_select_fusion
  2.0 0.8 exponential_multiply_fusion
  2.8 0.7 slice_bitcast_fusion
  3.5 9.9 %copy.40 = f32[4096,4,128]{0,2,1:T(8,128)} copy(f32[4096,4,128]{2,1,0:T(4,128)} %param.6) | data formatting | bytes 16777216 | tf_op args[0]
  13.4 4.3 %fusion.15 = f32[4096,4,128]{0,2,1:T(8,128)S(1)} fusion(f32[4096,4,128]{0,2,1:T(8,128)} %copy.40, f32[4096]{0:T(1024)S(1)} %get-tuple-element.64, f32[4,128]{1,0:T(4,128)S(1)} %compare_select_fusion, f32[4,128]{1,0:T(4,128)S(1)} %slice_bitcast_fusion, pred[4,128]{1,0:T(4,128)(4,1)S(1)} %get-tuple-element.11), kind=kLoop, calls=%fused_computation.24 | loop fusion | flops 6291456 | bytes 16798208 | tf_op jit(solution)/shard_map/jit(_where)/select_n | solution.py:188
  17.7 3.4 %copy-done = f32[4096,4,128]{0,2,1:T(8,128)} copy-done((f32[4096,4,128]{0,2,1:T(8,128)}, f32[4096,4,128]{0,2,1:T(8,128)S(1)}, u32[]{:S(2)}) %copy-start) | copy-done | bytes 8388632
  21.1 1.7 fusion.88
  22.8 4.5 %collective-permute-start = (f32[4096,1,128]{0,2,1:T(8,128)}, f32[4096,1,128]{0,2,1:T(8,128)}, u32[]{:S(2)}, u32[]{:S(2)}) collective-permute-start(f32[4096,1,128]{0,2,1:T(8,128)} %get-tuple-element.15), channel_id=1, source_target_pairs={{0,8},{8,16},{16,24},{1,9},{9,17},{17,25},{2,10},{10,18},{18,26},{... | collective-permute-start | bytes 6291464 | tf_op jit(solution)/shard_map/ppermute | solution.py:64
  27.4 1.9 %collective-permute-start.1 = (f32[4096,1,128]{0,2,1:T(8,128)S(1)}, f32[4096,1,128]{0,2,1:T(8,128)}, u32[]{:S(2)}, u32[]{:S(2)}) collective-permute-start(f32[4096,1,128]{0,2,1:T(8,128)S(1)} %get-tuple-element.16), channel_id=1, source_target_pairs={{8,0},{16,8},{24,16},{9,1},{17,9},{25,17},{10,2},{18,10},{26,18},{... | collective-permute-start | bytes 6291464 | tf_op jit(solution)/shard_map/ppermute | solution.py:66
  30.3 20.3 %collective-permute-done = f32[4096,1,128]{0,2,1:T(8,128)} collective-permute-done((f32[4096,1,128]{0,2,1:T(8,128)}, f32[4096,1,128]{0,2,1:T(8,128)}, u32[]{:S(2)}, u32[]{:S(2)}) %collective-permute-start) | collective-permute-done | bytes 2097184 | tf_op jit(solution)/shard_map/ppermute | solution.py:64
  50.6 4.2 %collective-permute-done.1 = f32[4096,1,128]{0,2,1:T(8,128)} collective-permute-done((f32[4096,1,128]{0,2,1:T(8,128)S(1)}, f32[4096,1,128]{0,2,1:T(8,128)}, u32[]{:S(2)}, u32[]{:S(2)}) %collective-permute-start.1) | collective-permute-done | bytes 2097184 | tf_op jit(solution)/shard_map/ppermute | solution.py:66
  54.8 25.5 %fusion.6 = f32[4096,4,128]{0,2,1:T(8,128)} fusion(f32[4096,4,128]{0,2,1:T(8,128)} %copy-done, f32[4096,1,128]{0,2,1:T(8,128)} %collective-permute-done.1, f32[4096,1,128]{0,2,1:T(8,128)} %collective-permute-done, f32[4096]{0:T(1024)S(1)} %get-tuple-element.57, f32[4096]{0:T(1024)S(1)} %get-tuple-element.55, f32[4096]{0:T(1024)S(1)} %get-tuple-element.61, ...), kind=kOutput, calls=%fused_computation.10 | convolution fusion | flops 383778816 | bytes 21291776 | tf_op jit(solution)/shard_map/dot_general | solution.py:208
  80.3 9.0 %fusion.13 = f32[13,4,128]{2,0,1:T(8,128)S(1)} fusion(f32[4096,4,128]{0,2,1:T(8,128)} %fusion.6, f32[13,4096]{1,0:T(8,128)S(1)} %stack.118, f32[4096]{0:T(1024)S(1)} %get-tuple-element.12), kind=kOutput, calls=%fused_computation.21 | convolution fusion | flops 327208960 | bytes 8644608 | tf_op jit(solution)/shard_map/dot_general | solution.py:214
  89.7 32.7 %psum.7 = f32[13,4,16,8]{2,3,0,1:T(8,128)S(1)} all-reduce(f32[13,4,16,8]{2,3,0,1:T(8,128)S(1)} %copy.44), channel_id=1, replica_groups=mesh['space'=4,'vel'=8] {'vel'}, use_global_device_ids=true, to_apply=%region_0.1 | all-reduce | flops 6656 | bytes 53248 | tf_op jit(solution)/shard_map/psum | solution.py:220
  122.4 1.9 %collective-permute-start.2 = (f32[13,1,16,8]{2,3,0,1:T(8,128)S(1)}, f32[13,1,16,8]{2,3,0,1:T(8,128)S(1)}, u32[]{:S(2)}, u32[]{:S(2)}) collective-permute-start(f32[13,1,16,8]{2,3,0,1:T(8,128)S(1)} %get-tuple-element.32), channel_id=1, source_target_pairs={{8,0},{16,8},{24,16},{9,1},{17,9},{25,17},{10,2},{18,10},{26,18},{... | collective-permute-start | bytes 19976 | tf_op jit(solution)/shard_map/ppermute | solution.py:66
  124.4 9.0 %collective-permute-start.3 = (f32[13,1,16,8]{2,3,0,1:T(8,128)S(1)}, f32[13,1,16,8]{2,3,0,1:T(8,128)S(1)}, u32[]{:S(2)}, u32[]{:S(2)}) collective-permute-start(f32[13,1,16,8]{2,3,0,1:T(8,128)S(1)} %get-tuple-element.31), channel_id=1, source_target_pairs={{0,8},{8,16},{16,24},{1,9},{9,17},{17,25},{2,10},{10,18},{18,26},{... | collective-permute-start | bytes 19976 | tf_op jit(solution)/shard_map/ppermute | solution.py:64
  133.8 0.7 collective-permute-done.3
  136.7 1.9 %collective-permute-start.4 = (f32[13,1,16,8]{2,3,0,1:T(8,128)S(1)}, f32[13,1,16,8]{2,3,0,1:T(8,128)S(1)}, u32[]{:S(2)}, u32[]{:S(2)}) collective-permute-start(f32[13,1,16,8]{2,3,0,1:T(8,128)S(1)} %get-tuple-element.30), channel_id=1, source_target_pairs={{8,0},{16,8},{24,16},{9,1},{17,9},{25,17},{10,2},{18,10},{26,18},{... | collective-permute-start | bytes 19976 | tf_op jit(solution)/shard_map/ppermute | solution.py:66
  138.6 4.3 %collective-permute-start.5 = (f32[13,1,16,8]{2,3,0,1:T(8,128)S(1)}, f32[13,1,16,8]{2,3,0,1:T(8,128)S(1)}, u32[]{:S(2)}, u32[]{:S(2)}) collective-permute-start(f32[13,1,16,8]{2,3,0,1:T(8,128)S(1)} %get-tuple-element.29), channel_id=1, source_target_pairs={{0,8},{8,16},{16,24},{1,9},{9,17},{17,25},{2,10},{10,18},{18,26},{... | collective-permute-start | bytes 19976 | tf_op jit(solution)/shard_map/ppermute | solution.py:64
  142.9 1.2 collective-permute-done.5
  146.3 1.9 %collective-permute-start.6 = (f32[13,1,16,8]{2,3,0,1:T(8,128)S(1)}, f32[13,1,16,8]{2,3,0,1:T(8,128)S(1)}, u32[]{:S(2)}, u32[]{:S(2)}) collective-permute-start(f32[13,1,16,8]{2,3,0,1:T(8,128)S(1)} %get-tuple-element.28), channel_id=1, source_target_pairs={{8,0},{16,8},{24,16},{9,1},{17,9},{25,17},{10,2},{18,10},{26,18},{... | collective-permute-start | bytes 19976 | tf_op jit(solution)/shard_map/ppermute | solution.py:66
  148.2 4.3 %collective-permute-start.7 = (f32[13,1,16,8]{2,3,0,1:T(8,128)S(1)}, f32[13,1,16,8]{2,3,0,1:T(8,128)S(1)}, u32[]{:S(2)}, u32[]{:S(2)}) collective-permute-start(f32[13,1,16,8]{2,3,0,1:T(8,128)S(1)} %get-tuple-element.27), channel_id=1, source_target_pairs={{0,8},{8,16},{16,24},{1,9},{9,17},{17,25},{2,10},{10,18},{18,26},{... | collective-permute-start | bytes 19976 | tf_op jit(solution)/shard_map/ppermute | solution.py:64
  152.5 1.2 collective-permute-done.7
  155.9 1.9 %collective-permute-start.8 = (f32[13,1,16,8]{2,3,0,1:T(8,128)S(1)}, f32[13,1,16,8]{2,3,0,1:T(8,128)S(1)}, u32[]{:S(2)}, u32[]{:S(2)}) collective-permute-start(f32[13,1,16,8]{2,3,0,1:T(8,128)S(1)} %get-tuple-element.26), channel_id=1, source_target_pairs={{8,0},{16,8},{24,16},{9,1},{17,9},{25,17},{10,2},{18,10},{26,18},{... | collective-permute-start | bytes 19976 | tf_op jit(solution)/shard_map/ppermute | solution.py:66
  157.8 4.5 %collective-permute-start.9 = (f32[13,1,16,8]{2,3,0,1:T(8,128)S(1)}, f32[13,1,16,8]{2,3,0,1:T(8,128)S(1)}, u32[]{:S(2)}, u32[]{:S(2)}) collective-permute-start(f32[13,1,16,8]{2,3,0,1:T(8,128)S(1)} %get-tuple-element.25), channel_id=1, source_target_pairs={{0,8},{8,16},{16,24},{1,9},{9,17},{17,25},{2,10},{10,18},{18,26},{... | collective-permute-start | bytes 19976 | tf_op jit(solution)/shard_map/ppermute | solution.py:64
  162.6 0.6 collective-permute-done.9
  163.3 0.6 fusion.26
  165.5 0.6 fusion.22
  167.1 11.1 %convolution_add_fusion = f32[4096,4,128]{0,2,1:T(8,128)} fusion(f32[4096,4,128]{0,2,1:T(8,128)} %fusion.6, f32[13,4096]{1,0:T(8,128)S(1)} %stack.108, f32[4,128,13]{1,0,2:T(4,128)S(1)} %dot_general.76), kind=kOutput, calls=%fused_computation.25 | convolution fusion | flops 329252864 | bytes 17016832 | tf_op jit(solution)/shard_map/dot_general | solution.py:230
  178.2 9.9 %copy.74 = f32[4096,4,128]{2,1,0:T(4,128)} copy(f32[4096,4,128]{0,2,1:T(8,128)} %convolution_add_fusion) | data formatting | bytes 16777216
  188.3 0.8 reshape.52
  (75 shorter events, 11.4 us)
Async XLA Ops:
  3.5 9.9 %copy-start.1 = (s32[4096]{0:T(1024)S(1)}, s32[4096]{0:T(1024)}, u32[]{:S(2)}) copy-start(s32[4096]{0:T(1024)} %param.7) | copy-start | bytes 49156
  17.7 3.4 %copy-start = (f32[4096,4,128]{0,2,1:T(8,128)}, f32[4096,4,128]{0,2,1:T(8,128)S(1)}, u32[]{:S(2)}) copy-start(f32[4096,4,128]{0,2,1:T(8,128)S(1)} %fusion.15) | copy-start | bytes 25165828
  21.1 8.2 %copy-start.5 = (f32[13,4,128]{2,1,0:T(4,128)S(1)}, f32[13,4,128]{2,1,0:T(4,128)}, u32[]{:S(2)}) copy-start(f32[13,4,128]{2,1,0:T(4,128)} %param.8) | copy-start | bytes 79876
  21.1 8.2 %copy-start.6 = (f32[4,128]{1,0:T(4,128)S(1)}, f32[4,128]{1,0:T(4,128)}, u32[]{:S(2)}) copy-start(f32[4,128]{1,0:T(4,128)} %param.9) | copy-start | bytes 6148
  22.8 27.8 %collective-permute-start = (f32[4096,1,128]{0,2,1:T(8,128)}, f32[4096,1,128]{0,2,1:T(8,128)}, u32[]{:S(2)}, u32[]{:S(2)}) collective-permute-start(f32[4096,1,128]{0,2,1:T(8,128)} %get-tuple-element.15), channel_id=1, source_target_pairs={{0,8},{8,16},{16,24},{1,9},{9,17},{17,25},{2,10},{10,18},{18,26},{... | collective-permute-start | bytes 6291464 | tf_op jit(solution)/shard_map/ppermute | solution.py:64
  27.4 27.5 %collective-permute-start.1 = (f32[4096,1,128]{0,2,1:T(8,128)S(1)}, f32[4096,1,128]{0,2,1:T(8,128)}, u32[]{:S(2)}, u32[]{:S(2)}) collective-permute-start(f32[4096,1,128]{0,2,1:T(8,128)S(1)} %get-tuple-element.16), channel_id=1, source_target_pairs={{8,0},{16,8},{24,16},{9,1},{17,9},{25,17},{10,2},{18,10},{26,18},{... | collective-permute-start | bytes 6291464 | tf_op jit(solution)/shard_map/ppermute | solution.py:66
  80.3 54.6 %copy-start.4 = (f32[13,13,1,1]{1,0,3,2:T(8,128)S(1)}, f32[13,13,1,1]{1,0,3,2:T(8,128)}, u32[]{:S(2)}) copy-start(f32[13,13,1,1]{1,0,3,2:T(8,128)} %constant.156) | copy-start | bytes 2032
  80.3 55.1 %copy-start.2 = (f32[13,13,1,1]{1,0,3,2:T(8,128)S(1)}, f32[13,13,1,1]{1,0,3,2:T(8,128)}, u32[]{:S(2)}) copy-start(f32[13,13,1,1]{1,0,3,2:T(8,128)} %constant.158) | copy-start | bytes 2032
  80.3 55.5 %copy-start.3 = (f32[13,13,1,1]{1,0,3,2:T(8,128)S(1)}, f32[13,13,1,1]{1,0,3,2:T(8,128)}, u32[]{:S(2)}) copy-start(f32[13,13,1,1]{1,0,3,2:T(8,128)} %constant.157) | copy-start | bytes 2032
  122.4 11.3 %collective-permute-start.2 = (f32[13,1,16,8]{2,3,0,1:T(8,128)S(1)}, f32[13,1,16,8]{2,3,0,1:T(8,128)S(1)}, u32[]{:S(2)}, u32[]{:S(2)}) collective-permute-start(f32[13,1,16,8]{2,3,0,1:T(8,128)S(1)} %get-tuple-element.32), channel_id=1, source_target_pairs={{8,0},{16,8},{24,16},{9,1},{17,9},{25,17},{10,2},{18,10},{26,18},{... | collective-permute-start | bytes 19976 | tf_op jit(solution)/shard_map/ppermute | solution.py:66
  124.4 10.1 %collective-permute-start.3 = (f32[13,1,16,8]{2,3,0,1:T(8,128)S(1)}, f32[13,1,16,8]{2,3,0,1:T(8,128)S(1)}, u32[]{:S(2)}, u32[]{:S(2)}) collective-permute-start(f32[13,1,16,8]{2,3,0,1:T(8,128)S(1)} %get-tuple-element.31), channel_id=1, source_target_pairs={{0,8},{8,16},{16,24},{1,9},{9,17},{17,25},{2,10},{10,18},{18,26},{... | collective-permute-start | bytes 19976 | tf_op jit(solution)/shard_map/ppermute | solution.py:64
  136.7 6.2 %collective-permute-start.4 = (f32[13,1,16,8]{2,3,0,1:T(8,128)S(1)}, f32[13,1,16,8]{2,3,0,1:T(8,128)S(1)}, u32[]{:S(2)}, u32[]{:S(2)}) collective-permute-start(f32[13,1,16,8]{2,3,0,1:T(8,128)S(1)} %get-tuple-element.30), channel_id=1, source_target_pairs={{8,0},{16,8},{24,16},{9,1},{17,9},{25,17},{10,2},{18,10},{26,18},{... | collective-permute-start | bytes 19976 | tf_op jit(solution)/shard_map/ppermute | solution.py:66
  138.6 5.5 %collective-permute-start.5 = (f32[13,1,16,8]{2,3,0,1:T(8,128)S(1)}, f32[13,1,16,8]{2,3,0,1:T(8,128)S(1)}, u32[]{:S(2)}, u32[]{:S(2)}) collective-permute-start(f32[13,1,16,8]{2,3,0,1:T(8,128)S(1)} %get-tuple-element.29), channel_id=1, source_target_pairs={{0,8},{8,16},{16,24},{1,9},{9,17},{17,25},{2,10},{10,18},{18,26},{... | collective-permute-start | bytes 19976 | tf_op jit(solution)/shard_map/ppermute | solution.py:64
  146.3 6.2 %collective-permute-start.6 = (f32[13,1,16,8]{2,3,0,1:T(8,128)S(1)}, f32[13,1,16,8]{2,3,0,1:T(8,128)S(1)}, u32[]{:S(2)}, u32[]{:S(2)}) collective-permute-start(f32[13,1,16,8]{2,3,0,1:T(8,128)S(1)} %get-tuple-element.28), channel_id=1, source_target_pairs={{8,0},{16,8},{24,16},{9,1},{17,9},{25,17},{10,2},{18,10},{26,18},{... | collective-permute-start | bytes 19976 | tf_op jit(solution)/shard_map/ppermute | solution.py:66
  148.2 5.5 %collective-permute-start.7 = (f32[13,1,16,8]{2,3,0,1:T(8,128)S(1)}, f32[13,1,16,8]{2,3,0,1:T(8,128)S(1)}, u32[]{:S(2)}, u32[]{:S(2)}) collective-permute-start(f32[13,1,16,8]{2,3,0,1:T(8,128)S(1)} %get-tuple-element.27), channel_id=1, source_target_pairs={{0,8},{8,16},{16,24},{1,9},{9,17},{17,25},{2,10},{10,18},{18,26},{... | collective-permute-start | bytes 19976 | tf_op jit(solution)/shard_map/ppermute | solution.py:64
  155.9 6.7 %collective-permute-start.8 = (f32[13,1,16,8]{2,3,0,1:T(8,128)S(1)}, f32[13,1,16,8]{2,3,0,1:T(8,128)S(1)}, u32[]{:S(2)}, u32[]{:S(2)}) collective-permute-start(f32[13,1,16,8]{2,3,0,1:T(8,128)S(1)} %get-tuple-element.26), channel_id=1, source_target_pairs={{8,0},{16,8},{24,16},{9,1},{17,9},{25,17},{10,2},{18,10},{26,18},{... | collective-permute-start | bytes 19976 | tf_op jit(solution)/shard_map/ppermute | solution.py:66
  157.8 5.5 %collective-permute-start.9 = (f32[13,1,16,8]{2,3,0,1:T(8,128)S(1)}, f32[13,1,16,8]{2,3,0,1:T(8,128)S(1)}, u32[]{:S(2)}, u32[]{:S(2)}) collective-permute-start(f32[13,1,16,8]{2,3,0,1:T(8,128)S(1)} %get-tuple-element.25), channel_id=1, source_target_pairs={{0,8},{8,16},{16,24},{1,9},{9,17},{17,25},{2,10},{10,18},{18,26},{... | collective-permute-start | bytes 19976 | tf_op jit(solution)/shard_map/ppermute | solution.py:64
where the time goes:
time: 190 us; the launch traced here: 189 us
  matrix products  51 us (27%)
  starting transfers between devices  36.2 us (19%)
  blocking collectives  32.7 us (17%)
  local copies, waits for them, and re-layouts  29.9 us (16%)
  waiting for transfers between devices  28.2 us (15%)
  other arithmetic  10.1 us (5%)
    psum x1, blocking collectives, local(): lax.psum(partial_value, 'vel').reshape(13, width_x, rows_y, NZ)  32.7 us
    ppermute x5, starting transfers between devices, padded_2(): lax.ppermute(tail, axis, [(i, (i + 1) % count) for i in range(ends)])  26.5 us
    dot_general x1, matrix products, local(): jnp.dot(equilibrium_rows.T, macro_state.reshape(13, -1), precision=lax.Pr...  25.5 us
    ppermute x5, waiting for transfers between devices, padded_2(): lax.ppermute(tail, axis, [(i, (i + 1) % count) for i in range(ends)])  24 us
    unnamed x18, local copies, waits for them, and re-layouts  23.2 us
    dot_general x1, matrix products, local(): jnp.dot(grad_rows.T, change.reshape(13, -1), precision=lax.Precision.HIGH...  11.1 us
    ppermute x5, starting transfers between devices, padded_2(): lax.ppermute(head, axis, [((i + 1) % count, i) for i in range(ends)])  9.6 us
    dot_general x1, matrix products, local(): jnp.dot(moment_rows, updated.reshape(slot_count, -1), precision=lax.Preci...  8.98 us
  transfers between devices with their start and end apart: 10, of which 6 were waited for; matrix products, arithmetic and copies ran while one was open for 1% of the time, Pallas kernels for 0%

commit v1 on v0

v1 whole, which is shorter than its diff:
```python
import functools
import math

import jax
import jax.numpy as jnp
import numpy as np
from jax import lax
from jax.experimental import pallas as pl
from jax.experimental.pallas import tpu as pltpu
from jax.sharding import PartitionSpec as P

SWEEPS = 4
LID_SPEED = 1.0
COUPLING = (
    (0, 1, 0, 0.24),
    (0, 2, 1, 0.24),
    (0, 3, 2, 0.24),
    (1, 0, 0, 0.2),
    (1, 4, 0, 0.2),
    (1, 5, 0, 0.2),
    (1, 7, 1, 0.1),
    (1, 8, 2, 0.1),
    (2, 0, 1, 0.2),
    (2, 4, 1, 0.2),
    (2, 6, 1, 0.2),
    (2, 7, 0, 0.1),
    (2, 9, 2, 0.1),
    (3, 0, 2, 0.2),
    (3, 4, 2, 0.2),
    (3, 8, 0, 0.1),
    (3, 9, 1, 0.1),
    (4, 10, 0, 0.2),
    (4, 11, 1, 0.2),
    (4, 12, 2, 0.2),
    (5, 1, 0, 0.4),
    (5, 10, 0, 0.2),
    (6, 2, 1, 0.4),
    (6, 11, 1, 0.2),
    (7, 1, 1, 0.2),
    (7, 2, 0, 0.2),
    (8, 1, 2, 0.2),
    (8, 3, 0, 0.2),
    (9, 2, 2, 0.2),
    (9, 3, 1, 0.2),
    (10, 4, 0, 0.5),
    (10, 5, 0, 0.2),
    (11, 4, 1, 0.5),
    (11, 6, 1, 0.2),
    (12, 4, 2, 0.5),
    (12, 8, 0, 0.1),
    (12, 9, 1, 0.1),
)


PLANES = 4
LANES = 128
SHIFT_Y = 8
SHIFT_Z = 1
CHUNK = 256
SUB = 128
COLS = 10
MESH = pl.DeviceIdType.MESH


def coupling_matrix():
    table = np.zeros((16, 48), np.float32)
    for row, column, dim, value in COUPLING:
        table[row, dim * 16 + column] = value
    return table


def split(x):
    high = x.astype(jnp.bfloat16)
    low = (x - high.astype(jnp.float32)).astype(jnp.bfloat16)
    return high, low


def store_rows(ref, rows):
    for k, row in enumerate(rows):
        ref[pl.ds(k, 1), :] = row


def transport_kernel(
    n_space, n_vel, chunks,
    dist_ref, order_ref, macro_ref, rate_ref, wall_ref, coupling_ref,
    upd_ref, grad_ref, change_ref, mom_ref,
    dist, halo, stage, upd, table, eq_t, mom_t, rhs, rhs_f, acc, fields, fields_src,
    rs_src, rs_dst, reduced, held,
    in_sem, out_sem, halo_send, halo_recv, fld_send, fld_recv, rs_send, rs_recv, ag_send, ag_recv,
):
    space = lax.axis_index("space")
    vel = lax.axis_index("vel")
    has_left = space > 0
    has_right = space < n_space - 1
    rows_part = 16 * PLANES // n_vel
    per_plane = n_vel // PLANES

    def in_copy(i):
        rows = pl.ds(i * (CHUNK * PLANES), CHUNK * PLANES)
        return pltpu.make_async_copy(dist_ref.at[rows, :], dist.at[i], in_sem.at[i])

    def load_chunk(c, carry):
        in_copy(c).start()
        in_copy(chunks + c).start()
        return carry

    lax.fori_loop(0, chunks, load_chunk, 0)

    barrier = pltpu.get_barrier_semaphore()
    for off in range(n_vel):
        peer = lax.rem(vel + off, n_vel)
        if off:
            pl.semaphore_signal(barrier, inc=1, device_id={"vel": peer}, device_id_type=MESH)

        @pl.when(has_left)
        def _():
            pl.semaphore_signal(
                barrier, inc=1, device_id={"space": space - 1, "vel": peer}, device_id_type=MESH
            )

        @pl.when(has_right)
        def _():
            pl.semaphore_signal(
                barrier, inc=1, device_id={"space": space + 1, "vel": peer}, device_id_type=MESH
            )

    fields_src[0:4, :] = rate_ref[...]
    fields_src[4:8, :] = wall_ref[...].astype(jnp.float32)
    fields_src[8:12, :] = macro_ref[0]
    fields_src[12:16, :] = jnp.zeros((4, LANES), jnp.float32)

    @pl.when(jnp.logical_not(has_left))
    def _():
        fields[0] = jnp.zeros((16, LANES), jnp.float32)
        held[0] = jnp.zeros(held.shape[1:], jnp.float32)
        halo[0:chunks] = jnp.zeros((chunks, CHUNK, LANES), jnp.float32)

    @pl.when(jnp.logical_not(has_right))
    def _():
        fields[1] = jnp.zeros((16, LANES), jnp.float32)
        held[2] = jnp.zeros(held.shape[1:], jnp.float32)
        halo[chunks : 2 * chunks] = jnp.zeros((chunks, CHUNK, LANES), jnp.float32)

    beside = jnp.minimum(space, 1) + jnp.minimum(n_space - 1 - space, 1)
    pl.semaphore_wait(barrier, n_vel - 1 + n_vel * beside)

    def fields_copy(side):
        return pltpu.make_async_remote_copy(
            fields_src, fields.at[side], fld_send.at[side], fld_recv.at[side],
            device_id={"space": space + 1 if side == 0 else space - 1}, device_id_type=MESH,
        )

    def halo_copy(side, i):
        return pltpu.make_async_remote_copy(
            stage.at[i], halo.at[i], halo_send.at[i], halo_recv.at[i],
            device_id={"space": space + 1 if side == 0 else space - 1}, device_id_type=MESH,
        )

    sends = (has_right, has_left)
    receives = (has_left, has_right)
    for side in range(2):

        @pl.when(sends[side])
        def _():
            fields_copy(side).start()

    def send_halo(c, carry):
        for side in range(2):
            i = side * chunks + c
            in_copy(i).wait()
            plane = PLANES - 1 if side == 0 else 0

            @pl.when(sends[side])
            def _():
                stage[i] = dist[i, pl.ds(plane, CHUNK, stride=PLANES), :]
                halo_copy(side, i).start()

        return carry

    lax.fori_loop(0, chunks, send_halo, 0)

    def make_tables(i, carry):
        order = order_ref[i]
        x = ((order >> 10) * 2 - 31).astype(jnp.float32) * 0.125
        y = (((order >> 5) & 31) * 2 - 31).astype(jnp.float32) * 0.125
        z = ((order & 31) * 2 - 31).astype(jnp.float32) * 0.125
        square = x * x + y * y + z * z
        one = jnp.ones_like(x)
        zero = jnp.zeros_like(x)
        energy = square - 1.5
        heat = square - 2.5
        store_rows(
            table,
            [one, x, y, z, energy, x * heat, y * heat, z * heat,
             jnp.abs(x), jnp.abs(y), jnp.abs(z),
             jnp.where(y > 0, 1.0, -1.0), jnp.where(z > 0, 1.0, -1.0), zero, zero, zero],
        )
        high, low = split(table[...])
        eq_t[i, 0:16, :] = high
        eq_t[i, 16:32, :] = low
        eq_t[i, 32:48, :] = high
        weight = jnp.exp(-square) * (0.25**3 / math.pi**1.5)
        third = square * (1.0 / 3.0)
        store_rows(
            table,
            [weight, weight * x, weight * y, weight * z, weight * energy * (2.0 / 3.0),
             2.0 * weight * (x * x - third), 2.0 * weight * (y * y - third),
             2.0 * weight * (x * y), 2.0 * weight * (x * z), 2.0 * weight * (y * z),
             weight * x * heat, weight * y * heat, weight * z * heat, zero, zero, zero],
        )
        high, low = split(table[...])
        mom_t[i, 0:16, :] = high
        mom_t[i, 16:32, :] = low
        store_rows(
            table,
            [one, 2.0 * x, 2.0 * y, 2.0 * z, energy, x * x - z * z, y * y - z * z,
             2.0 * x * y, 2.0 * x * z, 2.0 * y * z,
             0.8 * x * heat, 0.8 * y * heat, 0.8 * z * heat, zero, zero, zero],
        )
        high, low = split(table[...])
        grad_ref[i, 0:16, :] = high
        grad_ref[i, 16:32, :] = low
        grad_ref[i, 32:48, :] = high
        return carry

    lax.fori_loop(0, 2 * chunks, make_tables, 0)

    zero_row = jnp.zeros((1, LANES), jnp.float32)
    rhs_f[...] = jnp.zeros((16, COLS * LANES), jnp.float32)
    shakhov = 4.0 / 15.0
    for p in range(PLANES):
        rate = rate_ref[pl.ds(p, 1), :]
        wall = wall_ref[pl.ds(p, 1), :]
        gas = wall == 0
        moving = jnp.where(wall == 2, 2.0 * LID_SPEED, 0.0)
        for k, (source, scale) in enumerate(
            ((0, 1.0), (1, 2.0), (2, 2.0), (3, 2.0), (4, 1.0), (10, shakhov), (11, shakhov), (12, shakhov))
        ):
            value = macro_ref[source, pl.ds(p, 1), :]
            other = value if k == 0 else moving if k == 1 else zero_row
            rhs_f[pl.ds(k, 1), pl.ds(p * LANES, LANES)] = jnp.where(gas, rate * value * scale, other)
    lane = lax.broadcasted_iota(jnp.int32, (1, LANES), 1).astype(jnp.float32)
    one_row = jnp.ones((1, LANES), jnp.float32)
    for k in range(3):
        rhs_f[pl.ds(8 + k, 1), pl.ds((5 + k) * LANES, LANES)] = one_row
    for k, step in enumerate((SHIFT_Y, SHIFT_Z)):
        rhs_f[pl.ds(0, 1), pl.ds((8 + k) * LANES, LANES)] = lane
        rhs_f[pl.ds(11 + k, 1), pl.ds((8 + k) * LANES, LANES)] = one_row * (-1.0 * step)

    for side in range(2):

        @pl.when(receives[side])
        def _():
            fields_copy(side).wait_recv()

        plane = PLANES - 1 if side == 0 else 0
        wall_next = fields[side, pl.ds(4 + plane, 1), :]
        rhs_f[pl.ds(0, 1), pl.ds(4 * LANES, LANES)] = fields[side, pl.ds(8 + plane, 1), :]
        rhs_f[pl.ds(1, 1), pl.ds(4 * LANES, LANES)] = jnp.where(wall_next > 1.5, 2.0 * LID_SPEED, 0.0)
        high, low = split(rhs_f[...])
        rhs[side, 0:16, :] = high
        rhs[side, 16:32, :] = high
        rhs[side, 32:48, :] = low

    acc[...] = jnp.zeros(acc.shape, jnp.float32)

    def out_copy(i):
        slots = pl.ds(i * CHUNK, CHUNK)
        return pltpu.make_async_copy(upd.at[i], upd_ref.at[i], out_sem.at[i])

    def advance(side, i):
        @pl.when(receives[side])
        def _():
            halo_copy(side, i).wait_recv()

        for sub in range(CHUNK // SUB):
            first = sub * SUB
            lhs = eq_t[i, :, first : first + SUB]
            out = lax.dot_general(
                lhs, rhs[side], (((0,), (0,)), ((), ())), preferred_element_type=jnp.float32
            )
            cols = [out[:, k * LANES : (k + 1) * LANES] for k in range(COLS)]
            speed_x, speed_y, speed_z = cols[5:8]
            index_y = cols[8].astype(jnp.int32) & (LANES - 1)
            index_z = cols[9].astype(jnp.int32) & (LANES - 1)
            total = speed_x + speed_y + speed_z
            gas = [wall_ref[pl.ds(p, 1), :] == 0 for p in range(PLANES)]
            plane = PLANES - 1 if side == 0 else 0
            gas_next = fields[side, pl.ds(4 + plane, 1), :] == 0.0
            current = [
                jnp.where(gas[p], dist[i, pl.ds(first * PLANES + p, SUB, stride=PLANES), :], cols[p])
                for p in range(PLANES)
            ]
            beyond = jnp.where(gas_next, halo[i, first : first + SUB, :], cols[4])
            line = [beyond] + current[:-1] if side == 0 else current[1:] + [beyond]
            for p in range(PLANES):
                along_y = jnp.take_along_axis(current[p], index_y, axis=1, mode="promise_in_bounds")
                along_z = jnp.take_along_axis(current[p], index_z, axis=1, mode="promise_in_bounds")
                flow = cols[p] + speed_x * line[p] + speed_y * along_y + speed_z * along_z
                below = total + rate_ref[pl.ds(p, 1), :]
                guess = pl.reciprocal(below, approx=True)
                guess = guess * (2.0 - below * guess)
                value = jnp.where(gas[p], flow * guess, cols[p])
                upd[i, p, first : first + SUB, :] = value
                high, low = split(value)
                weights = mom_t[i, :, first : first + SUB]
                acc[:, p * LANES : (p + 1) * LANES] += jnp.dot(
                    jnp.concatenate([weights, weights], axis=1),
                    jnp.concatenate([high, low], axis=0),
                    preferred_element_type=jnp.float32,
                )
        out_copy(i).start()

    def step(c, carry):
        for side in range(2):
            advance(side, side * chunks + c)
        return carry

    lax.fori_loop(0, chunks, step, 0)

    for part in range(n_vel):
        plane, k = part // per_plane, part % per_plane
        first = k * rows_part
        lanes = pl.ds(plane * LANES, LANES)
        rs_src[part] = acc[pl.ds(first, rows_part), lanes] + acc[pl.ds(16 + first, rows_part), lanes]

    def rs_copy(off):
        peer = lax.rem(vel + off, n_vel)
        return pltpu.make_async_remote_copy(
            rs_src.at[peer], rs_dst.at[vel], rs_send.at[off], rs_recv.at[vel],
            device_id={"vel": peer}, device_id_type=MESH,
        )

    def rs_arrival(off):
        peer = lax.rem(vel + off, n_vel)
        return pltpu.make_async_remote_copy(
            rs_src.at[peer], rs_dst.at[peer], rs_send.at[off], rs_recv.at[peer],
            device_id={"vel": peer}, device_id_type=MESH,
        )

    for off in range(1, n_vel):
        rs_copy(off).start()
    rs_dst[vel] = rs_src[vel]
    for off in range(1, n_vel):
        rs_arrival(off).wait_recv()
    whole = rs_dst[0]
    for part in range(1, n_vel):
        whole = whole + rs_dst[part]
    reduced[...] = whole

    def ag_copy(shift, off):
        return pltpu.make_async_remote_copy(
            reduced, held.at[1 - shift, vel],
            ag_send.at[1 + shift, off], ag_recv.at[1 - shift, vel],
            device_id={"space": space + shift, "vel": lax.rem(vel + off, n_vel)}, device_id_type=MESH,
        )

    def ag_arrival(k, off):
        peer = lax.rem(vel + off, n_vel)
        return pltpu.make_async_remote_copy(
            reduced, held.at[k, peer],
            ag_send.at[k, off], ag_recv.at[k, peer],
            device_id={"space": space, "vel": peer}, device_id_type=MESH,
        )

    @pl.when(has_left)
    def _():
        for off in range(n_vel):
            ag_copy(-1, off).start()

    @pl.when(has_right)
    def _():
        for off in range(n_vel):
            ag_copy(1, off).start()

    for off in range(1, n_vel):
        ag_copy(0, off).start()
    held[1, vel] = whole
    for off in range(1, n_vel):
        ag_arrival(1, off).wait_recv()

    @pl.when(has_left)
    def _():
        for off in range(n_vel):
            ag_arrival(0, off).wait_recv()

    @pl.when(has_right)
    def _():
        for off in range(n_vel):
            ag_arrival(2, off).wait_recv()

    start = []
    for k in range(3):
        for p in range(PLANES):
            parts = [held[k, p * per_plane + m] for m in range(per_plane)]
            start.append(parts[0] if per_plane == 1 else jnp.concatenate(parts, axis=0))
    reaction, gas = [], []
    for k in range(3):
        for p in range(PLANES):
            source = fields_src if k == 1 else fields.at[0 if k == 0 else 1]
            reaction.append(1.0 + source[pl.ds(p, 1), :])
            gas.append(source[pl.ds(4 + p, 1), :] == 0.0)
    now = list(start)
    count = len(start)
    for sweep in range(1, SWEEPS + 1):
        inner = range(sweep, count - sweep)
        sums, differences = [], []
        for p in inner:
            up_y = pltpu.roll(now[p], LANES - SHIFT_Y, 1)
            down_y = pltpu.roll(now[p], SHIFT_Y, 1)
            up_z = pltpu.roll(now[p], LANES - SHIFT_Z, 1)
            down_z = pltpu.roll(now[p], SHIFT_Z, 1)
            sums.append(now[p + 1] + now[p - 1] + up_y + down_y + up_z + down_z)
            differences.append(
                jnp.concatenate([now[p + 1] - now[p - 1], up_y - down_y, up_z - down_z], axis=0)
            )
        high, low = split(jnp.concatenate(differences, axis=1))
        coupled = jnp.dot(
            coupling_ref[...],
            jnp.concatenate([high, high, low], axis=0),
            preferred_element_type=jnp.float32,
        )
        later = list(now)
        for m, p in enumerate(inner):
            value = reaction[p] * start[p] + sums[m] - 0.5 * coupled[:, m * LANES : (m + 1) * LANES]
            later[p] = jnp.where(gas[p], value / (reaction[p] + 6.0), start[p])
        now = later

    for p in range(PLANES):
        lanes = pl.ds(p * LANES, LANES)
        high, low = split(now[PLANES + p] - start[PLANES + p])
        change_ref[0:16, lanes] = high
        change_ref[16:32, lanes] = high
        change_ref[32:48, lanes] = low
        for k in range(13):
            mom_ref[k, pl.ds(p, 1), :] = now[PLANES + p][k : k + 1, :]

    def drain(c, carry):
        for side in range(2):
            i = side * chunks + c
            out_copy(i).wait()

            @pl.when(sends[side])
            def _():
                halo_copy(side, i).wait_send()

        return carry

    lax.fori_loop(0, chunks, drain, 0)
    for side in range(2):

        @pl.when(sends[side])
        def _():
            fields_copy(side).wait_send()

    for off in range(1, n_vel):
        rs_copy(off).wait_send()
        ag_copy(0, off).wait_send()

    @pl.when(has_left)
    def _():
        for off in range(n_vel):
            ag_copy(-1, off).wait_send()

    @pl.when(has_right)
    def _():
        for off in range(n_vel):
            ag_copy(1, off).wait_send()


def correct_kernel(group, upd_ref, grad_ref, change_ref, settled_ref, out_ref, mom_ref):
    @pl.when(pl.program_id(0) == 0)
    def _():
        mom_ref[...] = settled_ref[...]

    for i in range(group):
        change = lax.dot_general(
            grad_ref[i], change_ref[...], (((0,), (0,)), ((), ())), preferred_element_type=jnp.float32
        )
        for p in range(PLANES):
            rows = pl.ds(i * CHUNK * PLANES + p, CHUNK, stride=PLANES)
            out_ref[rows, :] = upd_ref[i, p] + change[:, p * LANES : (p + 1) * LANES]


def local(n_space, n_vel, distribution, velocity_order, macro_state, rarefaction, wall_mask):
    slots = distribution.shape[0]
    pieces = slots // CHUNK
    chunks = pieces // 2
    f32, bf16 = jnp.float32, jnp.bfloat16
    table = coupling_matrix()
    high = table.astype(bf16)
    low = (table - high.astype(np.float32)).astype(bf16)
    coupling = jnp.asarray(np.concatenate([high, low, high], axis=1))
    rows_part = 16 * PLANES // n_vel
    vmem = pl.BlockSpec(memory_space=pltpu.VMEM)
    hbm = pl.BlockSpec(memory_space=pl.ANY)
    dma = pltpu.SemaphoreType.DMA
    updated, grad, change, settled = pl.pallas_call(
        functools.partial(transport_kernel, n_space, n_vel, chunks),
        out_shape=(
            jax.ShapeDtypeStruct((pieces, PLANES, CHUNK, LANES), f32),
            jax.ShapeDtypeStruct((pieces, 48, CHUNK), bf16),
            jax.ShapeDtypeStruct((48, PLANES * LANES), bf16),
            jax.ShapeDtypeStruct((13, PLANES, LANES), f32),
        ),
        in_specs=[hbm, vmem, vmem, vmem, vmem, vmem],
        out_specs=(hbm, vmem, vmem, vmem),
        scratch_shapes=[
            pltpu.VMEM((pieces, CHUNK * PLANES, LANES), f32),
            pltpu.VMEM((pieces, CHUNK, LANES), f32),
            pltpu.VMEM((pieces, CHUNK, LANES), f32),
            pltpu.VMEM((pieces, PLANES, CHUNK, LANES), f32),
            pltpu.VMEM((16, CHUNK), f32),
            pltpu.VMEM((pieces, 48, CHUNK), bf16),
            pltpu.VMEM((pieces, 32, CHUNK), bf16),
            pltpu.VMEM((2, 48, COLS * LANES), bf16),
            pltpu.VMEM((16, COLS * LANES), f32),
            pltpu.VMEM((32, PLANES * LANES), f32),
            pltpu.VMEM((2, 16, LANES), f32),
            pltpu.VMEM((16, LANES), f32),
            pltpu.VMEM((n_vel, rows_part, LANES), f32),
            pltpu.VMEM((n_vel, rows_part, LANES), f32),
            pltpu.VMEM((rows_part, LANES), f32),
            pltpu.VMEM((3, n_vel, rows_part, LANES), f32),
            dma((pieces,)), dma((pieces,)), dma((pieces,)), dma((pieces,)),
            dma((2,)), dma((2,)), dma((n_vel,)), dma((n_vel,)), dma((3, n_vel)), dma((3, n_vel)),
        ],
        compiler_params=pltpu.CompilerParams(
            collective_id=0, has_side_effects=True, vmem_limit_bytes=48 * 2**20
        ),
        name="transport",
    )(
        distribution.reshape(slots * PLANES, LANES),
        velocity_order.reshape(pieces, 1, CHUNK),
        macro_state,
        rarefaction,
        wall_mask,
        coupling,
    )
    group = 2
    out, moments = pl.pallas_call(
        functools.partial(correct_kernel, group),
        grid=(pieces // group,),
        out_shape=(
            jax.ShapeDtypeStruct((slots * PLANES, LANES), f32),
            jax.ShapeDtypeStruct((13, PLANES, LANES), f32),
        ),
        in_specs=[
            pl.BlockSpec((group, PLANES, CHUNK, LANES), lambda g: (g, 0, 0, 0)),
            pl.BlockSpec((group, 48, CHUNK), lambda g: (g, 0, 0)),
            pl.BlockSpec((48, PLANES * LANES), lambda g: (0, 0)),
            pl.BlockSpec((13, PLANES, LANES), lambda g: (0, 0, 0)),
        ],
        out_specs=(
            pl.BlockSpec((group * CHUNK * PLANES, LANES), lambda g: (g, 0)),
            pl.BlockSpec((13, PLANES, LANES), lambda g: (0, 0, 0)),
        ),
        compiler_params=pltpu.CompilerParams(vmem_limit_bytes=32 * 2**20),
        name="correct",
    )(updated, grad, change, settled)
    return out.reshape(slots, PLANES, LANES), moments


def solution(mesh):
    return jax.shard_map(
        functools.partial(local, mesh.shape["space"], mesh.shape["vel"]),
        mesh=mesh,
        in_specs=(
            P("vel", "space", None),
            P("vel"),
            P(None, "space", None),
            P("space", None),
            P("space", None),
        ),
        out_specs=(P("vel", "space", None), P(None, "space", None)),
        check_vma=False,
    )
```

time: 190 us -> 54 us (0.28)
  matrix products: 51 us -> 0 us
  Pallas kernels: 0 us -> 46.1 us
  starting transfers between devices: 36.2 us -> 0 us
  blocking collectives: 32.7 us -> 0 us
  waiting for transfers between devices: 28.2 us -> 0 us
  local copies, waits for them, and re-layouts: 29.9 us -> 6.89 us
  other arithmetic: 10.1 us -> 0 us
    dot_general x15 -> x0, matrix products: 51 us -> none  [the longest x1 25.5 us: local(): jnp.dot(equilibrium_rows.T, macro_state.reshape(13, -1), precision=lax.Pr...]
    pallas_call x0 -> x2, Pallas kernels: none -> 46.1 us  [the longest x1 40.6 us: local(): pl.pallas_call(functools.partial(transport_kernel, n_space, n_vel, chunks...]
    ppermute x10 -> x0, starting transfers between devices: 36.2 us -> none  [the longest x5 26.5 us: padded_2(): lax.ppermute(tail, axis, [(i, (i + 1) % count) for i in range(ends)])]
    psum x1 -> x0, blocking collectives: 32.7 us -> none  [local(): lax.psum(partial_value, 'vel').reshape(13, width_x, rows_y, NZ)]
    ppermute x10 -> x0, waiting for transfers between devices: 28.2 us -> none  [the longest x5 24 us: padded_2(): lax.ppermute(tail, axis, [(i, (i + 1) % count) for i in range(ends)])]
    unnamed x18 -> x12, local copies, waits for them, and re-layouts: 23.2 us -> 6.89 us
    select_n x4 -> x0, other arithmetic: 5.63 us -> none  [the longest x1 4.29 us: local(): current = jnp.where(is_wall[None], wall_state, distribution)]
  transfers between devices with their start and end apart: 10 -> 0, of which waited for: 6 -> 0; matrix products, arithmetic and copies ran while one was open for 1% -> 0% of each run, Pallas kernels for 0% -> 0%
where the time goes in v1:
time: 54 us; the launch traced here: 53.7 us
  Pallas kernels  46.1 us (85%)
  local copies, waits for them, and re-layouts  6.89 us (13%)
  between operations  0.66 us (1%)
    pallas_call x1, Pallas kernels, local(): pl.pallas_call(functools.partial(transport_kernel, n_space, n_vel, chunks...  40.6 us
    unnamed x12, local copies, waits for them, and re-layouts  6.89 us
    pallas_call x1, Pallas kernels, local(): pl.pallas_call(functools.partial(correct_kernel, group), grid=(pieces //...  5.5 us

profile of v1, /device:TPU:1, one launch (start us, length us, event | category | flops | bytes accessed | tf_op | source)
XLA Modules:
  0.0 53.7 jit_solution(15581630409800535106)
XLA Ops:
  0.6 0.0 copy-start.1
  0.6 0.7 %copy-done.1 = f32[13,4,128]{2,1,0:T(4,128)S(1)} copy-done((f32[13,4,128]{2,1,0:T(4,128)S(1)}, f32[13,4,128]{2,1,0:T(4,128)}, u32[]{:S(2)}) %copy-start.1) | copy-done | bytes 26648
  1.4 0.0 copy-start.2
  1.4 0.7 %copy-done.2 = s32[4096]{0:T(1024)S(1)} copy-done((s32[4096]{0:T(1024)S(1)}, s32[4096]{0:T(1024)}, u32[]{:S(2)}) %copy-start.2) | copy-done | bytes 16408
  2.1 0.0 copy-start.3
  2.1 0.7 %copy-done.3 = bf16[16,144]{1,0:T(8,128)(2,1)S(1)} copy-done((bf16[16,144]{1,0:T(8,128)(2,1)S(1)}, bf16[16,144]{1,0:T(8,128)(2,1)}, u32[]{:S(2)}) %copy-start.3) | copy-done | bytes 4632
  2.8 0.0 copy-start.4
  2.8 0.7 %copy-done.4 = f32[4,128]{1,0:T(4,128)S(1)} copy-done((f32[4,128]{1,0:T(4,128)S(1)}, f32[4,128]{1,0:T(4,128)}, u32[]{:S(2)}) %copy-start.4) | copy-done | bytes 2072
  3.5 0.0 copy-start.5
  3.5 0.7 %copy-done.5 = s32[4,128]{1,0:T(4,128)S(1)} copy-done((s32[4,128]{1,0:T(4,128)S(1)}, s32[4,128]{1,0:T(4,128)}, u32[]{:S(2)}) %copy-start.5) | copy-done | bytes 2072
  4.2 40.6 %transport.1 = (f32[16,4,256,128]{3,2,1,0:T(8,128)}, bf16[16,48,256]{2,1,0:T(8,128)(2,1)S(1)}, bf16[48,512]{1,0:T(8,128)(2,1)S(1)}, f32[13,4,128]{2,1,0:T(4,128)S(1)}) custom-call(f32[16384,128]{1,0:T(8,128)} %bitcast.4, s32[16,1,256]{2,1,0:T(1,128)S(1)} %bitcast.3, f32[13,4,128]{2,1,0:T(4,128)S(1)} %copy-done.1, f32[4,128]{1,0:T(4,128)S(1)} %copy-done.4, ...), custom_call_target="tpu_custom_call" | custom-call | tf_op jit(solution)/shard_map/transport/pallas_call | solution.py:498
  44.8 0.0 copy-start
  44.8 3.4 %copy-done = f32[16,4,256,128]{3,2,1,0:T(8,128)S(1)} copy-done((f32[16,4,256,128]{3,2,1,0:T(8,128)S(1)}, f32[16,4,256,128]{3,2,1,0:T(8,128)}, u32[]{:S(2)}) %copy-start) | copy-done | bytes 8388632
  48.2 5.5 %correct.1 = (f32[16384,128]{1,0:T(8,128)}, f32[13,4,128]{2,1,0:T(4,128)}) custom-call(f32[16,4,256,128]{3,2,1,0:T(8,128)S(1)} %copy-done, bf16[16,48,256]{2,1,0:T(8,128)(2,1)S(1)} %get-tuple-element.9.grad_ref, bf16[48,512]{1,0:T(8,128)(2,1)S(1)} %get-tuple-element.10.change_ref, f32[13,4,128]{2,1,0:T(4,128)S(1)} %get-tuple-element.11.settled_ref), custom_call_target="tpu_custom_call" | custom-call | tf_op jit(solution)/shard_map/correct/pallas_call | solution.py:541
Async XLA Ops:
  0.6 0.7 %copy-start.1 = (f32[13,4,128]{2,1,0:T(4,128)S(1)}, f32[13,4,128]{2,1,0:T(4,128)}, u32[]{:S(2)}) copy-start(f32[13,4,128]{2,1,0:T(4,128)} %macro_ref.1) | copy-start | bytes 79876
  1.4 0.7 %copy-start.2 = (s32[4096]{0:T(1024)S(1)}, s32[4096]{0:T(1024)}, u32[]{:S(2)}) copy-start(s32[4096]{0:T(1024)} %param.7) | copy-start | bytes 49156
  2.1 0.7 %copy-start.3 = (bf16[16,144]{1,0:T(8,128)(2,1)S(1)}, bf16[16,144]{1,0:T(8,128)(2,1)}, u32[]{:S(2)}) copy-start(bf16[16,144]{1,0:T(8,128)(2,1)} %constant.2.clone.coupling_ref) | copy-start | bytes 13828
  2.8 0.7 %copy-start.4 = (f32[4,128]{1,0:T(4,128)S(1)}, f32[4,128]{1,0:T(4,128)}, u32[]{:S(2)}) copy-start(f32[4,128]{1,0:T(4,128)} %rate_ref.1) | copy-start | bytes 6148
  3.5 0.7 %copy-start.5 = (s32[4,128]{1,0:T(4,128)S(1)}, s32[4,128]{1,0:T(4,128)}, u32[]{:S(2)}) copy-start(s32[4,128]{1,0:T(4,128)} %wall_ref.1) | copy-start | bytes 6148
  44.8 3.4 %copy-start = (f32[16,4,256,128]{3,2,1,0:T(8,128)S(1)}, f32[16,4,256,128]{3,2,1,0:T(8,128)}, u32[]{:S(2)}) copy-start(f32[16,4,256,128]{3,2,1,0:T(8,128)} %get-tuple-element.8.upd_ref) | copy-start | bytes 25165828

commit v2 on v1

--- a/solution.py
+++ b/solution.py
@@ -62,13 +62,6 @@
 MESH = pl.DeviceIdType.MESH
 
 
-def coupling_matrix():
-    table = np.zeros((16, 48), np.float32)
-    for row, column, dim, value in COUPLING:
-        table[row, dim * 16 + column] = value
-    return table
-
-
 def split(x):
     high = x.astype(jnp.bfloat16)
     low = (x - high.astype(jnp.float32)).astype(jnp.bfloat16)
@@ -82,11 +75,12 @@
 
 def transport_kernel(
     n_space, n_vel, chunks,
-    dist_ref, order_ref, macro_ref, rate_ref, wall_ref, coupling_ref,
-    upd_ref, grad_ref, change_ref, mom_ref,
-    dist, halo, stage, upd, table, eq_t, mom_t, rhs, rhs_f, acc, fields, fields_src,
+    dist_ref, order_hbm, macro_hbm, rate_hbm, wall_hbm,
+    upd, grad_ref, change_ref, mom_ref,
+    order_ref, macro_ref, rate_ref, wall_ref,
+    dist, halo, stage, table, eq_t, mom_t, rhs, rhs_f, acc, fields, fields_src,
     rs_src, rs_dst, reduced, held,
-    in_sem, out_sem, halo_send, halo_recv, fld_send, fld_recv, rs_send, rs_recv, ag_send, ag_recv,
+    small_sem, in_sem, halo_send, halo_recv, fld_send, fld_recv, rs_send, rs_recv, ag_send, ag_recv,
 ):
     space = lax.axis_index("space")
     vel = lax.axis_index("vel")
@@ -95,6 +89,18 @@
     rows_part = 16 * PLANES // n_vel
     per_plane = n_vel // PLANES
 
+    small = [
+        pltpu.make_async_copy(source, target, small_sem.at[k])
+        for k, (source, target) in enumerate(
+            (
+                (rate_hbm, rate_ref), (wall_hbm, wall_ref), (macro_hbm, macro_ref),
+                (order_hbm, order_ref),
+            )
+        )
+    ]
+    for copy in small:
+        copy.start()
+
     def in_copy(i):
         rows = pl.ds(i * (CHUNK * PLANES), CHUNK * PLANES)
         return pltpu.make_async_copy(dist_ref.at[rows, :], dist.at[i], in_sem.at[i])
@@ -124,6 +130,9 @@
                 barrier, inc=1, device_id={"space": space + 1, "vel": peer}, device_id_type=MESH
             )
 
+    for copy in small[:3]:
+        copy.wait()
+
     fields_src[0:4, :] = rate_ref[...]
     fields_src[4:8, :] = wall_ref[...].astype(jnp.float32)
     fields_src[8:12, :] = macro_ref[0]
@@ -178,6 +187,8 @@
         return carry
 
     lax.fori_loop(0, chunks, send_halo, 0)
+
+    small[3].wait()
 
     def make_tables(i, carry):
         order = order_ref[i]
@@ -263,10 +274,6 @@
         rhs[side, 32:48, :] = low
 
     acc[...] = jnp.zeros(acc.shape, jnp.float32)
-
-    def out_copy(i):
-        slots = pl.ds(i * CHUNK, CHUNK)
-        return pltpu.make_async_copy(upd.at[i], upd_ref.at[i], out_sem.at[i])
 
     def advance(side, i):
         @pl.when(receives[side])
@@ -309,7 +316,6 @@
                     jnp.concatenate([high, low], axis=0),
                     preferred_element_type=jnp.float32,
                 )
-        out_copy(i).start()
 
     def step(c, carry):
         for side in range(2):
@@ -401,6 +407,13 @@
             reaction.append(1.0 + source[pl.ds(p, 1), :])
             gas.append(source[pl.ds(4 + p, 1), :] == 0.0)
     now = list(start)
+    row = lax.broadcasted_iota(jnp.int32, (16, 48), 0)
+    column = lax.broadcasted_iota(jnp.int32, (16, 48), 1)
+    weight = jnp.zeros((16, 48), jnp.float32)
+    for into, source, dim, value in COUPLING:
+        weight = jnp.where((row == into) & (column == dim * 16 + source), value, weight)
+    high, low = split(weight)
+    coupling = jnp.concatenate([high, low, high], axis=1)
     count = len(start)
     for sweep in range(1, SWEEPS + 1):
         inner = range(sweep, count - sweep)
@@ -416,7 +429,7 @@
             )
         high, low = split(jnp.concatenate(differences, axis=1))
         coupled = jnp.dot(
-            coupling_ref[...],
+            coupling,
             jnp.concatenate([high, high, low], axis=0),
             preferred_element_type=jnp.float32,
         )
@@ -438,8 +451,6 @@
     def drain(c, carry):
         for side in range(2):
             i = side * chunks + c
-            out_copy(i).wait()
-
             @pl.when(sends[side])
             def _():
                 halo_copy(side, i).wait_send()
@@ -473,13 +484,14 @@
     def _():
         mom_ref[...] = settled_ref[...]
 
+    base = pl.program_id(0) * group
     for i in range(group):
         change = lax.dot_general(
-            grad_ref[i], change_ref[...], (((0,), (0,)), ((), ())), preferred_element_type=jnp.float32
+            grad_ref[base + i], change_ref[...], (((0,), (0,)), ((), ())), preferred_element_type=jnp.float32
         )
         for p in range(PLANES):
             rows = pl.ds(i * CHUNK * PLANES + p, CHUNK, stride=PLANES)
-            out_ref[rows, :] = upd_ref[i, p] + change[:, p * LANES : (p + 1) * LANES]
+            out_ref[rows, :] = upd_ref[base + i, p] + change[:, p * LANES : (p + 1) * LANES]
 
 
 def local(n_space, n_vel, distribution, velocity_order, macro_state, rarefaction, wall_mask):
@@ -487,13 +499,9 @@
     pieces = slots // CHUNK
     chunks = pieces // 2
     f32, bf16 = jnp.float32, jnp.bfloat16
-    table = coupling_matrix()
-    high = table.astype(bf16)
-    low = (table - high.astype(np.float32)).astype(bf16)
-    coupling = jnp.asarray(np.concatenate([high, low, high], axis=1))
     rows_part = 16 * PLANES // n_vel
     vmem = pl.BlockSpec(memory_space=pltpu.VMEM)
-    hbm = pl.BlockSpec(memory_space=pl.ANY)
+    hbm = pl.BlockSpec(memory_space=pltpu.HBM)
     dma = pltpu.SemaphoreType.DMA
     updated, grad, change, settled = pl.pallas_call(
         functools.partial(transport_kernel, n_space, n_vel, chunks),
@@ -503,13 +511,16 @@
             jax.ShapeDtypeStruct((48, PLANES * LANES), bf16),
             jax.ShapeDtypeStruct((13, PLANES, LANES), f32),
         ),
-        in_specs=[hbm, vmem, vmem, vmem, vmem, vmem],
-        out_specs=(hbm, vmem, vmem, vmem),
+        in_specs=[hbm] * 5,
+        out_specs=(vmem,) * 4,
         scratch_shapes=[
+            pltpu.VMEM((pieces, 1, CHUNK), jnp.int32),
+            pltpu.VMEM((13, PLANES, LANES), f32),
+            pltpu.VMEM((PLANES, LANES), f32),
+            pltpu.VMEM((PLANES, LANES), jnp.int32),
             pltpu.VMEM((pieces, CHUNK * PLANES, LANES), f32),
             pltpu.VMEM((pieces, CHUNK, LANES), f32),
             pltpu.VMEM((pieces, CHUNK, LANES), f32),
-            pltpu.VMEM((pieces, PLANES, CHUNK, LANES), f32),
             pltpu.VMEM((16, CHUNK), f32),
             pltpu.VMEM((pieces, 48, CHUNK), bf16),
             pltpu.VMEM((pieces, 32, CHUNK), bf16),
@@ -522,11 +533,11 @@
             pltpu.VMEM((n_vel, rows_part, LANES), f32),
             pltpu.VMEM((rows_part, LANES), f32),
             pltpu.VMEM((3, n_vel, rows_part, LANES), f32),
-            dma((pieces,)), dma((pieces,)), dma((pieces,)), dma((pieces,)),
+            dma((4,)), dma((pieces,)), dma((pieces,)), dma((pieces,)),
             dma((2,)), dma((2,)), dma((n_vel,)), dma((n_vel,)), dma((3, n_vel)), dma((3, n_vel)),
         ],
         compiler_params=pltpu.CompilerParams(
-            collective_id=0, has_side_effects=True, vmem_limit_bytes=48 * 2**20
+            collective_id=0, has_side_effects=True, vmem_limit_bytes=40 * 2**20
         ),
         name="transport",
     )(
@@ -535,7 +546,6 @@
         macro_state,
         rarefaction,
         wall_mask,
-        coupling,
     )
     group = 2
     out, moments = pl.pallas_call(
@@ -546,10 +556,7 @@
             jax.ShapeDtypeStruct((13, PLANES, LANES), f32),
         ),
         in_specs=[
-            pl.BlockSpec((group, PLANES, CHUNK, LANES), lambda g: (g, 0, 0, 0)),
-            pl.BlockSpec((group, 48, CHUNK), lambda g: (g, 0, 0)),
-            pl.BlockSpec((48, PLANES * LANES), lambda g: (0, 0)),
-            pl.BlockSpec((13, PLANES, LANES), lambda g: (0, 0, 0)),
+            vmem, vmem, vmem, vmem,
         ],
         out_specs=(
             pl.BlockSpec((group * CHUNK * PLANES, LANES), lambda g: (g, 0)),

time: 54 us -> 49.8 us (0.922)
  local copies, waits for them, and re-layouts: 6.89 us -> 2.81 us
    unnamed x12 -> x8, local copies, waits for them, and re-layouts: 6.89 us -> 2.81 us
where the time goes in v2:
time: 49.8 us; the launch traced here: 49.5 us
  Pallas kernels  46 us (92%)
  local copies, waits for them, and re-layouts  2.81 us (6%)
  between operations  0.65 us (1%)
    pallas_call x1, Pallas kernels, local(): pl.pallas_call(functools.partial(transport_kernel, n_space, n_vel, chunks...  40.5 us
    pallas_call x1, Pallas kernels, local(): pl.pallas_call(functools.partial(correct_kernel, group), grid=(pieces //...  5.53 us
    unnamed x8, local copies, waits for them, and re-layouts  2.81 us

profile of v2, /device:TPU:1, one launch (start us, length us, event | category | flops | bytes accessed | tf_op | source)
XLA Modules:
  0.0 49.5 jit_solution(8925451551390913188)
XLA Ops:
  0.6 0.0 copy-start
  0.6 0.7 %copy-done = f32[13,4,128]{2,1,0:T(4,128)S(1)} copy-done((f32[13,4,128]{2,1,0:T(4,128)S(1)}, f32[13,4,128]{2,1,0:T(4,128)}, u32[]{:S(2)}) %copy-start) | copy-done | bytes 26648
  1.4 0.0 copy-start.1
  1.4 0.7 %copy-done.1 = s32[4096]{0:T(1024)S(1)} copy-done((s32[4096]{0:T(1024)S(1)}, s32[4096]{0:T(1024)}, u32[]{:S(2)}) %copy-start.1) | copy-done | bytes 16408
  2.1 0.0 copy-start.2
  2.1 0.7 %copy-done.2 = f32[4,128]{1,0:T(4,128)S(1)} copy-done((f32[4,128]{1,0:T(4,128)S(1)}, f32[4,128]{1,0:T(4,128)}, u32[]{:S(2)}) %copy-start.2) | copy-done | bytes 2072
  2.8 0.0 copy-start.3
  2.8 0.7 %copy-done.3 = s32[4,128]{1,0:T(4,128)S(1)} copy-done((s32[4,128]{1,0:T(4,128)S(1)}, s32[4,128]{1,0:T(4,128)}, u32[]{:S(2)}) %copy-start.3) | copy-done | bytes 2072
  3.5 40.5 %transport.1 = (f32[16,4,256,128]{3,2,1,0:T(8,128)S(1)}, bf16[16,48,256]{2,1,0:T(8,128)(2,1)S(1)}, bf16[48,512]{1,0:T(8,128)(2,1)S(1)}, f32[13,4,128]{2,1,0:T(4,128)S(1)}) custom-call(f32[16384,128]{1,0:T(8,128)} %bitcast.4, s32[16,1,256]{2,1,0:T(1,128)S(1)} %bitcast.3, f32[13,4,128]{2,1,0:T(4,128)S(1)} %copy-done, f32[4,128]{1,0:T(4,128)S(1)} %copy-done.2, ...), custom_call_target="tpu_custom_call" | custom-call | tf_op jit(solution)/shard_map/transport/pallas_call | solution.py:506
  44.0 5.5 %correct.1 = (f32[16384,128]{1,0:T(8,128)}, f32[13,4,128]{2,1,0:T(4,128)}) custom-call(f32[16,4,256,128]{3,2,1,0:T(8,128)S(1)} %get-tuple-element.8.upd_ref, bf16[16,48,256]{2,1,0:T(8,128)(2,1)S(1)} %get-tuple-element.9.grad_ref, bf16[48,512]{1,0:T(8,128)(2,1)S(1)} %get-tuple-element.10.change_ref, f32[13,4,128]{2,1,0:T(4,128)S(1)} %get-tuple-element.11.settled_ref), custom_call_target="tpu_custom_call" | custom-call | tf_op jit(solution)/shard_map/correct/pallas_call | solution.py:551
Async XLA Ops:
  0.6 0.7 %copy-start = (f32[13,4,128]{2,1,0:T(4,128)S(1)}, f32[13,4,128]{2,1,0:T(4,128)}, u32[]{:S(2)}) copy-start(f32[13,4,128]{2,1,0:T(4,128)} %macro_hbm.1) | copy-start | bytes 79876
  1.4 0.7 %copy-start.1 = (s32[4096]{0:T(1024)S(1)}, s32[4096]{0:T(1024)}, u32[]{:S(2)}) copy-start(s32[4096]{0:T(1024)} %param.6) | copy-start | bytes 49156
  2.1 0.7 %copy-start.2 = (f32[4,128]{1,0:T(4,128)S(1)}, f32[4,128]{1,0:T(4,128)}, u32[]{:S(2)}) copy-start(f32[4,128]{1,0:T(4,128)} %rate_hbm.1) | copy-start | bytes 6148
  2.8 0.7 %copy-start.3 = (s32[4,128]{1,0:T(4,128)S(1)}, s32[4,128]{1,0:T(4,128)}, u32[]{:S(2)}) copy-start(s32[4,128]{1,0:T(4,128)} %wall_hbm.1) | copy-start | bytes 6148

commit v3 on v2

--- a/solution.py
+++ b/solution.py
@@ -57,9 +57,13 @@
 SHIFT_Y = 8
 SHIFT_Z = 1
 CHUNK = 256
-SUB = 128
-COLS = 10
+SUB = 256
+COLS = 8
 MESH = pl.DeviceIdType.MESH
+
+
+def in_hbm(x):
+    return pltpu.with_memory_space_constraint(x, pltpu.HBM)
 
 
 def split(x):
@@ -203,8 +207,7 @@
         store_rows(
             table,
             [one, x, y, z, energy, x * heat, y * heat, z * heat,
-             jnp.abs(x), jnp.abs(y), jnp.abs(z),
-             jnp.where(y > 0, 1.0, -1.0), jnp.where(z > 0, 1.0, -1.0), zero, zero, zero],
+             zero, zero, zero, zero, zero, zero, zero, zero],
         )
         high, low = split(table[...])
         eq_t[i, 0:16, :] = high
@@ -250,13 +253,8 @@
             value = macro_ref[source, pl.ds(p, 1), :]
             other = value if k == 0 else moving if k == 1 else zero_row
             rhs_f[pl.ds(k, 1), pl.ds(p * LANES, LANES)] = jnp.where(gas, rate * value * scale, other)
-    lane = lax.broadcasted_iota(jnp.int32, (1, LANES), 1).astype(jnp.float32)
-    one_row = jnp.ones((1, LANES), jnp.float32)
     for k in range(3):
-        rhs_f[pl.ds(8 + k, 1), pl.ds((5 + k) * LANES, LANES)] = one_row
-    for k, step in enumerate((SHIFT_Y, SHIFT_Z)):
-        rhs_f[pl.ds(0, 1), pl.ds((8 + k) * LANES, LANES)] = lane
-        rhs_f[pl.ds(11 + k, 1), pl.ds((8 + k) * LANES, LANES)] = one_row * (-1.0 * step)
+        rhs_f[pl.ds(1 + k, 1), pl.ds((5 + k) * LANES, LANES)] = jnp.ones((1, LANES), jnp.float32)
 
     for side in range(2):
 
@@ -287,9 +285,8 @@
                 lhs, rhs[side], (((0,), (0,)), ((), ())), preferred_element_type=jnp.float32
             )
             cols = [out[:, k * LANES : (k + 1) * LANES] for k in range(COLS)]
-            speed_x, speed_y, speed_z = cols[5:8]
-            index_y = cols[8].astype(jnp.int32) & (LANES - 1)
-            index_z = cols[9].astype(jnp.int32) & (LANES - 1)
+            speed_x, speed_y, speed_z = (jnp.abs(col) for col in cols[5:8])
+            up_y, up_z = cols[6] > 0, cols[7] > 0
             total = speed_x + speed_y + speed_z
             gas = [wall_ref[pl.ds(p, 1), :] == 0 for p in range(PLANES)]
             plane = PLANES - 1 if side == 0 else 0
@@ -301,8 +298,13 @@
             beyond = jnp.where(gas_next, halo[i, first : first + SUB, :], cols[4])
             line = [beyond] + current[:-1] if side == 0 else current[1:] + [beyond]
             for p in range(PLANES):
-                along_y = jnp.take_along_axis(current[p], index_y, axis=1, mode="promise_in_bounds")
-                along_z = jnp.take_along_axis(current[p], index_z, axis=1, mode="promise_in_bounds")
+                cells = current[p]
+                along_y = jnp.where(
+                    up_y, pltpu.roll(cells, SHIFT_Y, 1), pltpu.roll(cells, LANES - SHIFT_Y, 1)
+                )
+                along_z = jnp.where(
+                    up_z, pltpu.roll(cells, SHIFT_Z, 1), pltpu.roll(cells, LANES - SHIFT_Z, 1)
+                )
                 flow = cols[p] + speed_x * line[p] + speed_y * along_y + speed_z * along_z
                 below = total + rate_ref[pl.ds(p, 1), :]
                 guess = pl.reciprocal(below, approx=True)
@@ -310,10 +312,9 @@
                 value = jnp.where(gas[p], flow * guess, cols[p])
                 upd[i, p, first : first + SUB, :] = value
                 high, low = split(value)
-                weights = mom_t[i, :, first : first + SUB]
-                acc[:, p * LANES : (p + 1) * LANES] += jnp.dot(
-                    jnp.concatenate([weights, weights], axis=1),
-                    jnp.concatenate([high, low], axis=0),
+                acc[:, 2 * p * LANES : 2 * (p + 1) * LANES] += jnp.dot(
+                    mom_t[i, :, first : first + SUB],
+                    jnp.concatenate([high, low], axis=1),
                     preferred_element_type=jnp.float32,
                 )
 
@@ -327,8 +328,9 @@
     for part in range(n_vel):
         plane, k = part // per_plane, part % per_plane
         first = k * rows_part
-        lanes = pl.ds(plane * LANES, LANES)
-        rs_src[part] = acc[pl.ds(first, rows_part), lanes] + acc[pl.ds(16 + first, rows_part), lanes]
+        tops, lows = pl.ds(first, rows_part), pl.ds(16 + first, rows_part)
+        high, low = pl.ds(2 * plane * LANES, LANES), pl.ds((2 * plane + 1) * LANES, LANES)
+        rs_src[part] = (acc[tops, high] + acc[tops, low]) + (acc[lows, high] + acc[lows, low])
 
     def rs_copy(off):
         peer = lax.rem(vel + off, n_vel)
@@ -526,7 +528,7 @@
             pltpu.VMEM((pieces, 32, CHUNK), bf16),
             pltpu.VMEM((2, 48, COLS * LANES), bf16),
             pltpu.VMEM((16, COLS * LANES), f32),
-            pltpu.VMEM((32, PLANES * LANES), f32),
+            pltpu.VMEM((32, 2 * PLANES * LANES), f32),
             pltpu.VMEM((2, 16, LANES), f32),
             pltpu.VMEM((16, LANES), f32),
             pltpu.VMEM((n_vel, rows_part, LANES), f32),
@@ -542,12 +544,12 @@
         name="transport",
     )(
         distribution.reshape(slots * PLANES, LANES),
-        velocity_order.reshape(pieces, 1, CHUNK),
-        macro_state,
-        rarefaction,
-        wall_mask,
+        in_hbm(velocity_order.reshape(pieces, 1, CHUNK)),
+        in_hbm(macro_state),
+        in_hbm(rarefaction),
+        in_hbm(wall_mask),
     )
-    group = 2
+    group = 4
     out, moments = pl.pallas_call(
         functools.partial(correct_kernel, group),
         grid=(pieces // group,),

time: 49.8 us -> 40 us (0.80)
  Pallas kernels: 46 us -> 39.2 us
  local copies, waits for them, and re-layouts: 2.81 us -> 0 us
    pallas_call x1, Pallas kernels: 40.5 us -> 34.9 us  [local(): pl.pallas_call(functools.partial(transport_kernel, n_space, n_vel, chunks...]
    unnamed x8 -> x0, local copies, waits for them, and re-layouts: 2.81 us -> none
    pallas_call x1, Pallas kernels: 5.53 us -> 4.28 us  [local(): pl.pallas_call(functools.partial(correct_kernel, group), grid=(pieces //...]
where the time goes in v3:
time: 40 us; the launch traced here: 39.9 us
  Pallas kernels  39.2 us (98%)
  between operations  0.64 us (2%)
    pallas_call x1, Pallas kernels, local(): pl.pallas_call(functools.partial(transport_kernel, n_space, n_vel, chunks...  34.9 us
    pallas_call x1, Pallas kernels, local(): pl.pallas_call(functools.partial(correct_kernel, group), grid=(pieces //...  4.28 us

profile of v3, /device:TPU:1, one launch (start us, length us, event | category | flops | bytes accessed | tf_op | source)
XLA Modules:
  0.0 39.9 jit_solution(2476354074436739902)
XLA Ops:
  0.6 34.9 %transport.1 = (f32[16,4,256,128]{3,2,1,0:T(8,128)S(1)}, bf16[16,48,256]{2,1,0:T(8,128)(2,1)S(1)}, bf16[48,512]{1,0:T(8,128)(2,1)S(1)}, f32[13,4,128]{2,1,0:T(4,128)S(1)}) custom-call(f32[16384,128]{1,0:T(8,128)} %bitcast.3, s32[16,1,256]{2,1,0:T(1,128)} %bitcast.4, f32[13,4,128]{2,1,0:T(4,128)} %macro_hbm.1, f32[4,128]{1,0:T(4,128)} %rate_hbm.1, ...), custom_call_target="tpu_custom_call" | custom-call | tf_op jit(solution)/shard_map/transport/pallas_call | solution.py:508
  35.6 4.3 %correct.1 = (f32[16384,128]{1,0:T(8,128)}, f32[13,4,128]{2,1,0:T(4,128)}) custom-call(f32[16,4,256,128]{3,2,1,0:T(8,128)S(1)} %get-tuple-element.8.upd_ref, bf16[16,48,256]{2,1,0:T(8,128)(2,1)S(1)} %get-tuple-element.9.grad_ref, bf16[48,512]{1,0:T(8,128)(2,1)S(1)} %get-tuple-element.10.change_ref, f32[13,4,128]{2,1,0:T(4,128)S(1)} %get-tuple-element.11.settled_ref), custom_call_target="tpu_custom_call" | custom-call | tf_op jit(solution)/shard_map/correct/pallas_call | solution.py:553

commit v4 on v3

--- a/solution.py
+++ b/solution.py
@@ -56,7 +56,7 @@
 LANES = 128
 SHIFT_Y = 8
 SHIFT_Z = 1
-CHUNK = 256
+CHUNK = 512
 SUB = 256
 COLS = 8
 MESH = pl.DeviceIdType.MESH
@@ -318,12 +318,20 @@
                     preferred_element_type=jnp.float32,
                 )
 
-    def step(c, carry):
+    near = 1 - lax.rem(space, 2)
+
+    def step(k, carry):
+        c = lax.rem(k, chunks)
+        turn = lax.rem(k // chunks + near, 2)
         for side in range(2):
-            advance(side, side * chunks + c)
+
+            @pl.when(turn == side)
+            def _():
+                advance(side, side * chunks + c)
+
         return carry
 
-    lax.fori_loop(0, chunks, step, 0)
+    lax.fori_loop(0, 2 * chunks, step, 0)
 
     for part in range(n_vel):
         plane, k = part // per_plane, part % per_plane
@@ -549,7 +557,7 @@
         in_hbm(rarefaction),
         in_hbm(wall_mask),
     )
-    group = 4
+    group = 2
     out, moments = pl.pallas_call(
         functools.partial(correct_kernel, group),
         grid=(pieces // group,),

time: 40 us -> 37.7 us (0.943)
  Pallas kernels: 39.2 us -> 36.9 us
    pallas_call x1, Pallas kernels: 34.9 us -> 32.6 us  [local(): pl.pallas_call(functools.partial(transport_kernel, n_space, n_vel, chunks...]
where the time goes in v4:
time: 37.7 us; the launch traced here: 37.5 us
  Pallas kernels  36.9 us (98%)
  between operations  0.64 us (2%)
    pallas_call x1, Pallas kernels, local(): pl.pallas_call(functools.partial(transport_kernel, n_space, n_vel, chunks...  32.6 us
    pallas_call x1, Pallas kernels, local(): pl.pallas_call(functools.partial(correct_kernel, group), grid=(pieces //...  4.28 us

profile of v4, /device:TPU:1, one launch (start us, length us, event | category | flops | bytes accessed | tf_op | source)
XLA Modules:
  0.0 37.5 jit_solution(2729855397036660309)
XLA Ops:
  0.6 32.6 %transport.1 = (f32[8,4,512,128]{3,2,1,0:T(8,128)S(1)}, bf16[8,48,512]{2,1,0:T(8,128)(2,1)S(1)}, bf16[48,512]{1,0:T(8,128)(2,1)S(1)}, f32[13,4,128]{2,1,0:T(4,128)S(1)}) custom-call(f32[16384,128]{1,0:T(8,128)} %bitcast.3, s32[8,1,512]{2,1,0:T(1,128)} %bitcast.4, f32[13,4,128]{2,1,0:T(4,128)} %macro_hbm.1, f32[4,128]{1,0:T(4,128)} %rate_hbm.1, s32[4,128]{1,0:T(4,128)} %wall_hbm.1), custom_call_target="tpu_custom_call" | custom-call | tf_op jit(solution)/shard_map/transport/pallas_call | solution.py:516
  33.2 4.3 %correct.1 = (f32[16384,128]{1,0:T(8,128)}, f32[13,4,128]{2,1,0:T(4,128)}) custom-call(f32[8,4,512,128]{3,2,1,0:T(8,128)S(1)} %get-tuple-element.8.upd_ref, bf16[8,48,512]{2,1,0:T(8,128)(2,1)S(1)} %get-tuple-element.9.grad_ref, bf16[48,512]{1,0:T(8,128)(2,1)S(1)} %get-tuple-element.10.change_ref, f32[13,4,128]{2,1,0:T(4,128)S(1)} %get-tuple-element.11.settled_ref), custom_call_target="tpu_custom_call" | custom-call | tf_op jit(solution)/shard_map/correct/pallas_call | solution.py:561
